TPU v7x, 32 devices: a whole 2x2x4 slice. The times are simulated.
32 devices in a mesh: ens: 2 (over x), lon: 16 (over z, y, core).
Axes of the slice: x: 2, y: 2, z: 4, core: 2. Of those that a mesh axis runs over, the one named last changes fastest.
Arguments:
- increment: float32 [4, 4, 128, 512], P(None, None, ('ens', 'lon')), parts along dimension 2, may hold values from -12 to 12
- coeffs: float32 [3, 4, 128, 512], P(None, None, ('ens', 'lon')), parts along dimension 2, may hold values from 0.02 to 0.3
- polar_rows: int32 [64], P('ens'), parts along dimension 0, may hold values from 0 to 511, as said below
- polar_weight: float32 [64], P('ens'), parts along dimension 0, may hold values from 0.2 to 0.8
- block_index: int32 [512], P(('ens', 'lon')), parts along dimension 0, may hold values from 0 to 63
- send_dest: int32 [512], P(('ens', 'lon')), parts along dimension 0, may hold values from 0 to 15, as said below
- slot_count: int32 [512], P(('ens', 'lon')), parts along dimension 0, may hold values from 0 to 2, as said below
- jacobian: float32 [1024, 8, 512], P(('ens', 'lon')), parts along dimension 0, may hold values from -2 to 2
- observed: float32 [1024, 8], P(('ens', 'lon')), parts along dimension 0, may hold values from -6 to 6
- obs_weight: float32 [1024, 8], P(('ens', 'lon')), parts along dimension 0, may hold values from 0.25 to 4
- bg_weight: float32 [4, 4], replicated, may hold values from 0.02 to 0.1
Outputs:
- gradient: float32 [4, 4, 128, 512], P(None, None, ('ens', 'lon')), parts along dimension 2
- model_state: float32 [4, 4, 128, 512], P(None, None, ('ens', 'lon')), parts along dimension 2
- obs_residual: float32 [1024, 8], P(('ens', 'lon')), parts along dimension 0
There are 2 independent parts, one for each index of `ens`. A program takes and returns all parts, laid end to end along the dimension named above; an argument that names none is the same for every part. Nothing has to cross between parts.
Inputs may be any that keep to these rules, and one draw needn't show every extreme that they name: `polar_rows`: 32 distinct latitudes, half among the 32 lowest and half among the 32 highest. `send_dest`: each device sends exactly 16 blocks and at most 2 to one owner; some owner receives 2 from every device. `slot_count`: entry o * 16 + s counts the sends of device s to owner o.
All inputs are finite; a program needn't handle non-finite values.
Results may differ from a plain program's by a relative error of at most 0.0001.
Values sent between devices are 32-bit elements; how exact they have to be, the bound alone decides.
A program may use at most 128 MiB of HBM per device.

v0:
```python
import jax
import jax.numpy as jnp
from jax import lax
from jax.sharding import PartitionSpec as P

STEPS = 4
CAP = 2


def shifted(block, axis, distance):
    devices = range(lax.axis_size(axis))
    route = [((i - distance) % len(devices), i) for i in devices]
    return lax.ppermute(block, axis, route)


def advance_local(padded, coeffs):
    west_c, north_c, south_c = (coeffs[0], coeffs[1], coeffs[2])
    centre = padded[:, :, 1:]
    west_cells = padded[:, :, :-1]
    zero_edge = jnp.zeros_like(centre[..., :1])
    north_cells = jnp.concatenate([centre[..., 1:], zero_edge], axis=3)
    south_cells = jnp.concatenate([zero_edge, centre[..., :-1]], axis=3)
    return (
        (1.0 - west_c - north_c - south_c) * centre
        + west_c * west_cells
        + north_c * north_cells
        + south_c * south_cells
    )


def polar_blend(field_in, polar_rows, polar_weight, columns):
    polar_vals = field_in[..., polar_rows]
    partial_value = jnp.sum(polar_vals, axis=2)
    zonal_sum = lax.psum(partial_value, "lon")
    zonal_mean = zonal_sum / (columns * lax.axis_size("lon"))
    blended = (1.0 - polar_weight) * polar_vals + polar_weight * zonal_mean[:, :, None, :]
    return field_in.at[..., polar_rows].set(blended)


def retreat_local(adjoint_in, coeffs):
    west_c, north_c, south_c = (coeffs[0], coeffs[1], coeffs[2])
    east_flux = west_c * adjoint_in
    east_edge = shifted(east_flux[:, :, :1], "lon", -1)
    from_east = jnp.concatenate([east_flux[:, :, 1:], east_edge], axis=2)
    zero_edge = jnp.zeros_like(adjoint_in[..., :1])
    north_flux = north_c * adjoint_in
    south_flux = south_c * adjoint_in
    north_in = jnp.concatenate([zero_edge, north_flux[..., :-1]], axis=3)
    south_in = jnp.concatenate([south_flux[..., 1:], zero_edge], axis=3)
    return (1.0 - west_c - north_c - south_c) * adjoint_in + from_east + north_in + south_in


def shards(
    increment,
    coeffs,
    polar_rows,
    polar_weight,
    block_index,
    send_dest,
    slot_count,
    jacobian,
    observed,
    obs_weight,
    bg_weight,
):
    columns = increment.shape[2]
    lat_cells = increment.shape[3]
    device_count = lax.axis_size("lon")
    model_state = increment
    for repeat in range(STEPS):
        west_edge = shifted(model_state[:, :, -1:], "lon", 1)
        padded = jnp.concatenate([west_edge, model_state], axis=2)
        model_state = polar_blend(advance_local(padded, coeffs), polar_rows, polar_weight, columns)
    blocks = model_state.reshape(-1, lat_cells)
    sent_blocks = blocks[block_index]
    same_dest = send_dest[:, None] == send_dest[None, :]
    position = jnp.arange(send_dest.shape[0], dtype=jnp.int32)
    earlier = position[None, :] < position[:, None]
    rank_in = jnp.sum((same_dest & earlier).astype(jnp.int32), axis=1)
    slot_row = send_dest * CAP + rank_in
    outgoing = jnp.zeros((device_count * CAP, lat_cells), jnp.float32).at[slot_row].set(sent_blocks)
    received = lax.all_to_all(outgoing, "lon", split_axis=0, concat_axis=0, tiled=True)
    model_obs = jnp.einsum("soc,sc->so", jacobian, received, precision=lax.Precision.HIGHEST)
    live_mask = (
        (jnp.arange(CAP, dtype=jnp.int32)[None, :] < slot_count[:, None])
        .astype(jnp.float32)
        .reshape(-1, 1)
    )
    weighted = obs_weight * live_mask
    misfit = model_obs - observed
    bias_term = jnp.sum(weighted * misfit) / (1.0 + jnp.sum(weighted))
    residual = weighted * (misfit - bias_term)
    returned = jnp.einsum("soc,so->sc", jacobian, residual, precision=lax.Precision.HIGHEST)
    returned_rows = lax.all_to_all(returned, "lon", split_axis=0, concat_axis=0, tiled=True)
    contrib = returned_rows[slot_row]
    adjoint = jnp.zeros_like(blocks).at[block_index].add(contrib).reshape(model_state.shape)
    for repeat in range(STEPS):
        adjoint = retreat_local(polar_blend(adjoint, polar_rows, polar_weight, columns), coeffs)
    gradient = bg_weight[:, :, None, None] * increment + adjoint
    return (gradient, model_state, residual)


def solution(mesh):
    placed = (
        P(None, None, ("ens", "lon"), None),
        P(None, None, ("ens", "lon"), None),
        P("ens"),
        P("ens"),
        P(("ens", "lon")),
        P(("ens", "lon")),
        P(("ens", "lon")),
        P(("ens", "lon"), None, None),
        P(("ens", "lon"), None),
        P(("ens", "lon"), None),
        P(),
    )
    return jax.shard_map(
        shards,
        mesh=mesh,
        in_specs=placed,
        out_specs=(
            P(None, None, ("ens", "lon"), None),
            P(None, None, ("ens", "lon"), None),
            P(("ens", "lon"), None),
        ),
        check_vma=False,
    )
```

profile of v0, /device:TPU:0, one launch (start us, length us, event | category | flops | bytes accessed | tf_op | source)
XLA Modules:
  0.0 853.7 jit_solution(2343139794600207057)
XLA Ops:
  19.7 7.3 multiply_add_fusion.3
  30.1 62.6 %psum.56 = f32[4,4,32]{1,0,2:T(4,128)S(1)} all-reduce(f32[4,4,32]{1,0,2:T(4,128)S(1)} %bitcast_reduce_fusion.7), channel_id=1, replica_groups=mesh['ens'=2,'lon'=16] {'lon'}, use_global_device_ids=true, to_apply=%region_2.0 | all-reduce | flops 512 | bytes 4096 | tf_op jit(solution)/shard_map/psum | solution.py:34
  93.1 3.8 scatter_fusion
  96.9 6.5 slice.182
  103.4 4.3 fusion.42
  111.3 4.5 broadcast_multiply_fusion.6
  126.0 7.3 multiply_add_fusion.2
  136.5 62.4 %psum.57 = f32[4,4,32]{1,0,2:T(4,128)S(1)} all-reduce(f32[4,4,32]{1,0,2:T(4,128)S(1)} %bitcast_reduce_fusion.6), channel_id=1, replica_groups=mesh['ens'=2,'lon'=16] {'lon'}, use_global_device_ids=true, to_apply=%region_5.0 | all-reduce | flops 512 | bytes 4096 | tf_op jit(solution)/shard_map/psum | solution.py:34
  199.2 3.8 scatter_fusion.1
  203.1 6.5 slice.185
  209.6 4.3 fusion.41
  217.5 4.5 broadcast_multiply_fusion.5
  232.2 7.3 multiply_add_fusion.1
  242.7 62.0 %psum.58 = f32[4,4,32]{1,0,2:T(4,128)S(1)} all-reduce(f32[4,4,32]{1,0,2:T(4,128)S(1)} %bitcast_reduce_fusion.5), channel_id=1, replica_groups=mesh['ens'=2,'lon'=16] {'lon'}, use_global_device_ids=true, to_apply=%region_8.0 | all-reduce | flops 512 | bytes 4096 | tf_op jit(solution)/shard_map/psum | solution.py:34
  305.0 3.8 scatter_fusion.2
  308.9 6.5 slice.188
  315.4 4.3 fusion.40
  323.7 4.5 broadcast_multiply_fusion.4
  338.4 7.3 multiply_add_fusion
  348.9 62.0 %psum.59 = f32[4,4,32]{1,0,2:T(4,128)S(1)} all-reduce(f32[4,4,32]{1,0,2:T(4,128)S(1)} %bitcast_reduce_fusion.4), channel_id=1, replica_groups=mesh['ens'=2,'lon'=16] {'lon'}, use_global_device_ids=true, to_apply=%region_11.0 | all-reduce | flops 512 | bytes 4096 | tf_op jit(solution)/shard_map/psum | solution.py:34
  411.3 3.8 scatter_fusion.3
  423.8 6.7 all-to-all-done
  452.7 61.9 %psum.60 = f32[4,4,32]{1,0,2:T(4,128)S(1)} all-reduce(f32[4,4,32]{1,0,2:T(4,128)S(1)} %bitcast_reduce_fusion.3), channel_id=1, replica_groups=mesh['ens'=2,'lon'=16] {'lon'}, use_global_device_ids=true, to_apply=%region_18.0 | all-reduce | flops 512 | bytes 4096 | tf_op jit(solution)/shard_map/psum | solution.py:34
  515.0 3.8 scatter_fusion.4
  518.8 4.5 broadcast_multiply_fusion.3
  527.1 7.0 slice_multiply_fusion.7
  534.1 4.2 slice.191
  541.4 10.3 %fusion.1 = f32[4,4,4,512]{2,1,3,0:T(4,128)} fusion(f32[4,4,1,512]{2,1,3,0:T(4,128)} %copy.146, f32[4,4,3,512]{2,1,3,0:T(4,128)} %slice.191, f32[4,4,4,511]{2,1,3,0:T(4,128)} %get-tuple-element.27, f32[4,4,4,511]{2,1,3,0:T(4,128)} %get-tuple-element.26, f32[4,4,4,512]{2,1,3,0:T(4,128)} %scatter_fusion.4, f32[4,4,512]{1,0,2:T(4,128)S(1)} %copy.115), kind=kLoop, calls=%fused_computation.22 | loop fusion | flops 163840 | bytes 687616 | tf_op jit(solution)/shard_map/add | solution.py:50
  555.0 58.0 %psum.61 = f32[4,4,32]{1,0,2:T(4,128)S(1)} all-reduce(f32[4,4,32]{1,0,2:T(4,128)S(1)} %bitcast_reduce_fusion.2), channel_id=1, replica_groups=mesh['ens'=2,'lon'=16] {'lon'}, use_global_device_ids=true, to_apply=%region_21.0 | all-reduce | flops 512 | bytes 4096 | tf_op jit(solution)/shard_map/psum | solution.py:34
  613.3 3.8 scatter_fusion.5
  617.2 4.5 broadcast_multiply_fusion
  625.4 7.0 slice_multiply_fusion.5
  632.4 4.1 slice.197
  639.8 10.4 %fusion.3 = f32[4,4,4,512]{2,1,3,0:T(4,128)} fusion(f32[4,4,1,512]{2,1,3,0:T(4,128)} %copy.148, f32[4,4,3,512]{2,1,3,0:T(4,128)} %slice.197, f32[4,4,4,511]{2,1,3,0:T(4,128)} %get-tuple-element.25, f32[4,4,4,511]{2,1,3,0:T(4,128)} %get-tuple-element.24, f32[4,4,4,512]{2,1,3,0:T(4,128)} %scatter_fusion.5, f32[4,4,512]{1,0,2:T(4,128)S(1)} %copy.115), kind=kLoop, calls=%fused_computation.25 | loop fusion | flops 163840 | bytes 687616 | tf_op jit(solution)/shard_map/add | solution.py:50
  653.3 58.0 %psum.62 = f32[4,4,32]{1,0,2:T(4,128)S(1)} all-reduce(f32[4,4,32]{1,0,2:T(4,128)S(1)} %bitcast_reduce_fusion.1), channel_id=1, replica_groups=mesh['ens'=2,'lon'=16] {'lon'}, use_global_device_ids=true, to_apply=%region_24.0 | all-reduce | flops 512 | bytes 4096 | tf_op jit(solution)/shard_map/psum | solution.py:34
  711.6 3.8 scatter_fusion.6
  715.4 4.5 broadcast_multiply_fusion.1
  723.7 7.0 slice_multiply_fusion.3
  730.8 4.1 slice.203
  738.1 10.3 %fusion.5 = f32[4,4,4,512]{2,1,3,0:T(4,128)} fusion(f32[4,4,1,512]{2,1,3,0:T(4,128)} %copy.150, f32[4,4,3,512]{2,1,3,0:T(4,128)} %slice.203, f32[4,4,4,511]{2,1,3,0:T(4,128)} %get-tuple-element.23, f32[4,4,4,511]{2,1,3,0:T(4,128)} %get-tuple-element.22, f32[4,4,4,512]{2,1,3,0:T(4,128)} %scatter_fusion.6, f32[4,4,512]{1,0,2:T(4,128)S(1)} %copy.115), kind=kLoop, calls=%fused_computation.28 | loop fusion | flops 163840 | bytes 687616 | tf_op jit(solution)/shard_map/add | solution.py:50
  751.6 57.9 %psum.63 = f32[4,4,32]{1,0,2:T(4,128)S(1)} all-reduce(f32[4,4,32]{1,0,2:T(4,128)S(1)} %bitcast_reduce_fusion), channel_id=1, replica_groups=mesh['ens'=2,'lon'=16] {'lon'}, use_global_device_ids=true, to_apply=%region_27.0 | all-reduce | flops 512 | bytes 4096 | tf_op jit(solution)/shard_map/psum | solution.py:34
  809.8 3.8 scatter_fusion.7
  813.7 4.5 broadcast_multiply_fusion.2
  818.1 3.6 copy.165
  822.1 6.8 slice_multiply_fusion.1
  828.9 4.2 slice.209
  836.3 12.5 %fusion.8 = f32[4,4,4,512]{2,1,3,0:T(4,128)} fusion(f32[4,4,4,512]{2,1,3,0:T(4,128)} %copy.153, f32[4,4,1,512]{2,1,3,0:T(4,128)} %copy.152, f32[4,4,3,512]{2,1,3,0:T(4,128)} %slice.209, f32[4,4,4,511]{2,1,3,0:T(4,128)} %get-tuple-element.21, f32[4,4,4,511]{2,1,3,0:T(4,128)} %get-tuple-element.20, f32[4,4,4,512]{2,1,3,0:T(4,128)} %scatter_fusion.7, ...), kind=kLoop, calls=%fused_computation.32 | loop fusion | flops 196608 | bytes 818688 | tf_op jit(solution)/shard_map/add | solution.py:99
  848.8 4.4 copy.154
  (151 shorter events, 139.8 us)
Async XLA Ops:
  0.6 430.0 %copy-start = (f32[32,8,512]{2,1,0:T(8,128)S(1)}, f32[32,8,512]{2,1,0:T(8,128)}, u32[]{:S(2)}) copy-start(f32[32,8,512]{2,1,0:T(8,128)} %param.18) | copy-start | bytes 1572868
  1.7 14.7 %collective-permute-start = (f32[4,4,1,512]{3,1,2,0:T(4,128)S(1)}, f32[4,4,1,512]{3,1,2,0:T(4,128)S(1)}, u32[]{:S(2)}, u32[]{:S(2)}) collective-permute-start(f32[4,4,1,512]{3,1,2,0:T(4,128)S(1)} %slice.181), channel_id=1, source_target_pairs={{15,0},{0,1},{1,2},{2,3},{3,4},{4,5},{5,6},{6,7},{7,8},{8,9},{9,10... | collective-permute-start | bytes 98312 | tf_op jit(solution)/shard_map/ppermute | solution.py:13
  9.5 6.9 copy-start.10
  9.5 6.9 copy-start.15
  96.9 6.5 copy-start.2
  111.2 11.6 %collective-permute-start.1 = (f32[4,4,1,512]{3,1,2,0:T(4,128)S(1)}, f32[4,4,1,512]{3,1,2,0:T(4,128)S(1)}, u32[]{:S(2)}, u32[]{:S(2)}) collective-permute-start(f32[4,4,1,512]{3,1,2,0:T(4,128)S(1)} %copy.127), channel_id=1, source_target_pairs={{15,0},{0,1},{1,2},{2,3},{3,4},{4,5},{5,6},{6,7},{7,8},{8,9},{9,10... | collective-permute-start | bytes 98312 | tf_op jit(solution)/shard_map/ppermute | solution.py:13
  203.1 6.5 copy-start.3
  217.4 11.6 %collective-permute-start.2 = (f32[4,4,1,512]{3,1,2,0:T(4,128)S(1)}, f32[4,4,1,512]{3,1,2,0:T(4,128)S(1)}, u32[]{:S(2)}, u32[]{:S(2)}) collective-permute-start(f32[4,4,1,512]{3,1,2,0:T(4,128)S(1)} %copy.132), channel_id=1, source_target_pairs={{15,0},{0,1},{1,2},{2,3},{3,4},{4,5},{5,6},{6,7},{7,8},{8,9},{9,10... | collective-permute-start | bytes 98312 | tf_op jit(solution)/shard_map/ppermute | solution.py:13
  308.9 6.5 copy-start.4
  323.2 12.0 %collective-permute-start.3 = (f32[4,4,1,512]{3,1,2,0:T(4,128)S(1)}, f32[4,4,1,512]{3,1,2,0:T(4,128)S(1)}, u32[]{:S(2)}, u32[]{:S(2)}) collective-permute-start(f32[4,4,1,512]{3,1,2,0:T(4,128)S(1)} %copy.137), channel_id=1, source_target_pairs={{15,0},{0,1},{1,2},{2,3},{3,4},{4,5},{5,6},{6,7},{7,8},{8,9},{9,10... | collective-permute-start | bytes 98312 | tf_op jit(solution)/shard_map/ppermute | solution.py:13
  345.7 77.9 %copy-start.16 = (s32[16]{0:T(128)S(1)}, s32[16]{0:T(128)}, u32[]{:S(2)}) copy-start(s32[16]{0:T(128)} %param.17) | copy-start | bytes 196
  345.7 86.0 %copy-start.12 = (f32[32,8]{0,1:T(8,128)S(1)}, f32[32,8]{0,1:T(8,128)}, u32[]{:S(2)}) copy-start(f32[32,8]{0,1:T(8,128)} %param.20) | copy-start | bytes 3076
  345.7 86.0 %copy-start.13 = (f32[32,8]{0,1:T(8,128)S(1)}, f32[32,8]{0,1:T(8,128)}, u32[]{:S(2)}) copy-start(f32[32,8]{0,1:T(8,128)} %param.19) | copy-start | bytes 3076
  418.6 26.9 %copy-start.11 = (f32[4,4,4,512]{3,2,1,0:T(4,128)}, f32[4,4,4,512]{3,2,1,0:T(4,128)S(1)}, u32[]{:S(2)}) copy-start(f32[4,4,4,512]{3,2,1,0:T(4,128)S(1)} %copy.142) | copy-start | bytes 393220
  420.1 10.4 %all-to-all-start = ((f32[16,2,512]{2,1,0:T(2,128)}), f32[16,2,512]{2,1,0:T(2,128)S(1)}, u32[]{:S(2)}, u32[]{:S(2)}) async-start(f32[16,2,512]{2,1,0:T(2,128)} %all_to_all.16), calls=%async_computation | async-start | bytes 131072 | tf_op jit(solution)/shard_map/all_to_all | solution.py:82
  433.7 11.8 %copy-start.14 = (f32[32,8]{0,1:T(8,128)}, f32[32,8]{0,1:T(8,128)S(1)}, u32[]{:S(2)}) copy-start(f32[32,8]{0,1:T(8,128)S(1)} %subtract_multiply_fusion) | copy-start | bytes 3076
  435.0 10.5 %all-to-all-start.1 = ((f32[16,2,512]{2,1,0:T(2,128)}), f32[16,2,512]{2,1,0:T(2,128)S(1)}, u32[]{:S(2)}, u32[]{:S(2)}) async-start(f32[16,2,512]{2,1,0:T(2,128)} %all_to_all.19), calls=%async_computation.1 | async-start | bytes 131072 | tf_op jit(solution)/shard_map/all_to_all | solution.py:94
  526.8 7.2 copy-start.6
  526.8 11.4 %collective-permute-start.4 = (f32[4,4,1,512]{3,1,2,0:T(4,128)S(1)}, f32[4,4,1,512]{3,1,2,0:T(4,128)S(1)}, u32[]{:S(2)}, u32[]{:S(2)}) collective-permute-start(f32[4,4,1,512]{3,1,2,0:T(4,128)S(1)} %copy.162), channel_id=1, source_target_pairs={{1,0},{2,1},{3,2},{4,3},{5,4},{6,5},{7,6},{8,7},{9,8},{10,9},{11,1... | collective-permute-start | bytes 98312 | tf_op jit(solution)/shard_map/ppermute | solution.py:13
  625.1 7.3 copy-start.7
  625.1 11.4 %collective-permute-start.5 = (f32[4,4,1,512]{3,1,2,0:T(4,128)S(1)}, f32[4,4,1,512]{3,1,2,0:T(4,128)S(1)}, u32[]{:S(2)}, u32[]{:S(2)}) collective-permute-start(f32[4,4,1,512]{3,1,2,0:T(4,128)S(1)} %copy.163), channel_id=1, source_target_pairs={{1,0},{2,1},{3,2},{4,3},{5,4},{6,5},{7,6},{8,7},{9,8},{10,9},{11,1... | collective-permute-start | bytes 98312 | tf_op jit(solution)/shard_map/ppermute | solution.py:13
  723.4 7.3 copy-start.8
  723.4 11.5 %collective-permute-start.6 = (f32[4,4,1,512]{3,1,2,0:T(4,128)S(1)}, f32[4,4,1,512]{3,1,2,0:T(4,128)S(1)}, u32[]{:S(2)}, u32[]{:S(2)}) collective-permute-start(f32[4,4,1,512]{3,1,2,0:T(4,128)S(1)} %copy.164), channel_id=1, source_target_pairs={{1,0},{2,1},{3,2},{4,3},{5,4},{6,5},{7,6},{8,7},{9,8},{10,9},{11,1... | collective-permute-start | bytes 98312 | tf_op jit(solution)/shard_map/ppermute | solution.py:13
  818.1 4.0 copy-start.9
  821.8 7.2 copy-start.5
  821.8 11.4 %collective-permute-start.7 = (f32[4,4,1,512]{3,1,2,0:T(4,128)S(1)}, f32[4,4,1,512]{3,1,2,0:T(4,128)S(1)}, u32[]{:S(2)}, u32[]{:S(2)}) collective-permute-start(f32[4,4,1,512]{3,1,2,0:T(4,128)S(1)} %copy.165), channel_id=1, source_target_pairs={{1,0},{2,1},{3,2},{4,3},{5,4},{6,5},{7,6},{8,7},{9,8},{10,9},{11,1... | collective-permute-start | bytes 98312 | tf_op jit(solution)/shard_map/ppermute | solution.py:13
  836.3 16.9 %copy-start.1 = (f32[32,8,512]{2,1,0:T(8,128)S(1)}, f32[32,8,512]{2,1,0:T(8,128)}, u32[]{:S(2)}) copy-start(f32[32,8,512]{2,1,0:T(8,128)} %param.18) | copy-start | bytes 1572868
where the time goes:
time: 864 us; the launch traced here: 854 us
  blocking collectives  485 us (56%)
  local copies, waits for them, and re-layouts  206 us (24%)
  other arithmetic  143 us (17%)
  starting transfers between devices  9.22 us (1%)
    psum x8, blocking collectives, polar_blend(): zonal_sum = lax.psum(partial_value, 'lon')  485 us
    scatter x12, local copies, waits for them, and re-layouts, polar_blend(): return field_in.at[..., polar_rows].set(blended)  44.7 us
    add x3, other arithmetic, retreat_local(): (1.0 - west_c - north_c - south_c) * adjoint_in + from_east + north_in  31 us
    slice x7, local copies, waits for them, and re-layouts, shards(): west_edge = shifted(model_state[:, :, -1:], 'lon', 1)  30.2 us
    add x8, other arithmetic, advance_local(): (1.0 - west_c - north_c - south_c) * centre + west_c * west_cells  29.3 us
    mul x4, other arithmetic, retreat_local(): north_flux = north_c * adjoint_in  27.8 us
    unnamed x43, local copies, waits for them, and re-layouts  26.1 us
    gather x8, local copies, waits for them, and re-layouts, polar_blend(): polar_vals = field_in[..., polar_rows]  23.5 us
  transfers between devices with their start and end apart: 10, of which 1 were waited for; matrix products, arithmetic and copies ran while one was open for 12% of the time, Pallas kernels for 0%

commit v1 on v0

--- a/solution.py
+++ b/solution.py
@@ -31,7 +31,7 @@
 def polar_blend(field_in, polar_rows, polar_weight, columns):
     polar_vals = field_in[..., polar_rows]
     partial_value = jnp.sum(polar_vals, axis=2)
-    zonal_sum = lax.psum(partial_value, "lon")
+    zonal_sum = jnp.sum(lax.all_gather(partial_value, "lon"), axis=0)
     zonal_mean = zonal_sum / (columns * lax.axis_size("lon"))
     blended = (1.0 - polar_weight) * polar_vals + polar_weight * zonal_mean[:, :, None, :]
     return field_in.at[..., polar_rows].set(blended)

time: 864 us -> 540 us (0.62)
  blocking collectives: 485 us -> 158 us
    psum x8 -> x0, blocking collectives: 485 us -> none  [polar_blend(): zonal_sum = lax.psum(partial_value, 'lon')]
    all_gather x0 -> x8, blocking collectives: none -> 158 us  [polar_blend(): zonal_sum = jnp.sum(lax.all_gather(partial_value, 'lon'), axis=0)]
  transfers between devices with their start and end apart: 10 -> 10, of which waited for: 1 -> 1; matrix products, arithmetic and copies ran while one was open for 12% -> 19% of each run, Pallas kernels for 0% -> 0%
where the time goes in v1:
time: 540 us; the launch traced here: 530 us
  local copies, waits for them, and re-layouts  208 us (39%)
  blocking collectives  158 us (29%)
  other arithmetic  142 us (26%)
  starting transfers between devices  10.5 us (2%)
  waiting for transfers between devices  6.71 us (1%)
    all_gather x8, blocking collectives, polar_blend(): zonal_sum = jnp.sum(lax.all_gather(partial_value, 'lon'), axis=0)  158 us
    scatter x12, local copies, waits for them, and re-layouts, polar_blend(): return field_in.at[..., polar_rows].set(blended)  44.7 us
    add x3, other arithmetic, retreat_local(): (1.0 - west_c - north_c - south_c) * adjoint_in + from_east + north_in  31 us
    slice x7, local copies, waits for them, and re-layouts, shards(): west_edge = shifted(model_state[:, :, -1:], 'lon', 1)  30.2 us
    add x8, other arithmetic, advance_local(): (1.0 - west_c - north_c - south_c) * centre + west_c * west_cells  29.3 us
    mul x4, other arithmetic, retreat_local(): north_flux = north_c * adjoint_in  28 us
    unnamed x43, local copies, waits for them, and re-layouts  26.1 us
    gather x8, local copies, waits for them, and re-layouts, polar_blend(): polar_vals = field_in[..., polar_rows]  23.5 us
  transfers between devices with their start and end apart: 10, of which 1 were waited for; matrix products, arithmetic and copies ran while one was open for 19% of the time, Pallas kernels for 0%

profile of v1, /device:TPU:0, one launch (start us, length us, event | category | flops | bytes accessed | tf_op | source)
XLA Modules:
  0.0 529.7 jit_solution(4198422170302313990)
XLA Ops:
  19.7 7.3 %multiply_add_fusion.3 = f32[4,4,4,512]{2,1,3,0:T(4,128)} fusion(f32[4,4,4,511]{2,1,3,0:T(4,128)} %copy.251, f32[4,4,4,512]{2,1,3,0:T(4,128)} %copy.198, f32[4,4,4,511]{2,1,3,0:T(4,128)} %copy.250, f32[4,4,512]{1,0,2:T(4,128)} %copy.199, f32[4,4,512]{1,0,2:T(4,128)S(1)} %copy.196), kind=kLoop, calls=%fused_computation.36 | loop fusion | flops 131072 | bytes 589312 | tf_op jit(solution)/shard_map/add | solution.py:24
  30.2 23.0 %all-gather = f32[64,4,32]{2,1,0:T(4,128)S(1)} all-gather(f32[4,4,32]{2,1,0:T(4,128)S(1)} %copy.201), channel_id=2, replica_groups=mesh['ens'=2,'lon'=16] {'lon'}, dimensions={0}, use_global_device_ids=true | all-gather | bytes 34816 | tf_op jit(solution)/shard_map/all_gather | solution.py:34
  53.6 3.8 scatter_fusion
  57.4 6.5 %slice.182 = f32[4,4,1,512]{2,1,3,0:T(4,128)} slice(f32[4,4,4,512]{2,1,3,0:T(4,128)} %scatter_fusion), slice={[0:4], [0:4], [3:4], [0:512]} | slice | bytes 65536 | tf_op jit(solution)/shard_map/slice | solution.py:71
  64.0 4.3 fusion.42
  72.2 4.5 broadcast_multiply_fusion.6
  86.9 7.3 %multiply_add_fusion.2 = f32[4,4,4,512]{2,1,3,0:T(4,128)} fusion(f32[4,4,4,511]{2,1,3,0:T(4,128)} %get-tuple-element.36, f32[4,4,4,512]{2,1,3,0:T(4,128)} %copy.207, f32[4,4,4,511]{2,1,3,0:T(4,128)} %get-tuple-element.35, f32[4,4,512]{1,0,2:T(4,128)} %copy.199, f32[4,4,512]{1,0,2:T(4,128)S(1)} %copy.196), kind=kLoop, calls=%fused_computation.35 | loop fusion | flops 131072 | bytes 589312 | tf_op jit(solution)/shard_map/add | solution.py:24
  97.5 18.2 %all-gather.1 = f32[64,4,32]{2,1,0:T(4,128)S(1)} all-gather(f32[4,4,32]{2,1,0:T(4,128)S(1)} %copy.208), channel_id=3, replica_groups=mesh['ens'=2,'lon'=16] {'lon'}, dimensions={0}, use_global_device_ids=true | all-gather | bytes 34816 | tf_op jit(solution)/shard_map/all_gather | solution.py:34
  116.1 3.8 scatter_fusion.1
  119.9 6.5 %slice.185 = f32[4,4,1,512]{2,1,3,0:T(4,128)} slice(f32[4,4,4,512]{2,1,3,0:T(4,128)} %scatter_fusion.1), slice={[0:4], [0:4], [3:4], [0:512]} | slice | bytes 65536 | tf_op jit(solution)/shard_map/slice | solution.py:71
  126.5 4.3 fusion.41
  134.5 4.5 broadcast_multiply_fusion.5
  149.2 7.3 %multiply_add_fusion.1 = f32[4,4,4,512]{2,1,3,0:T(4,128)} fusion(f32[4,4,4,511]{2,1,3,0:T(4,128)} %get-tuple-element.34, f32[4,4,4,512]{2,1,3,0:T(4,128)} %copy.214, f32[4,4,4,511]{2,1,3,0:T(4,128)} %get-tuple-element.33, f32[4,4,512]{1,0,2:T(4,128)} %copy.199, f32[4,4,512]{1,0,2:T(4,128)S(1)} %copy.196), kind=kLoop, calls=%fused_computation.34 | loop fusion | flops 131072 | bytes 589312 | tf_op jit(solution)/shard_map/add | solution.py:24
  159.8 19.1 %all-gather.2 = f32[64,4,32]{2,1,0:T(4,128)S(1)} all-gather(f32[4,4,32]{2,1,0:T(4,128)S(1)} %copy.215), channel_id=4, replica_groups=mesh['ens'=2,'lon'=16] {'lon'}, dimensions={0}, use_global_device_ids=true | all-gather | bytes 34816 | tf_op jit(solution)/shard_map/all_gather | solution.py:34
  179.3 3.8 scatter_fusion.2
  183.1 6.5 %slice.188 = f32[4,4,1,512]{2,1,3,0:T(4,128)} slice(f32[4,4,4,512]{2,1,3,0:T(4,128)} %scatter_fusion.2), slice={[0:4], [0:4], [3:4], [0:512]} | slice | bytes 65536 | tf_op jit(solution)/shard_map/slice | solution.py:71
  189.6 4.3 fusion.40
  198.2 4.5 broadcast_multiply_fusion.4
  213.0 7.3 %multiply_add_fusion = f32[4,4,4,512]{2,1,3,0:T(4,128)} fusion(f32[4,4,4,511]{2,1,3,0:T(4,128)} %get-tuple-element.32, f32[4,4,4,512]{2,1,3,0:T(4,128)} %copy.221, f32[4,4,4,511]{2,1,3,0:T(4,128)} %get-tuple-element.31, f32[4,4,512]{1,0,2:T(4,128)} %copy.199, f32[4,4,512]{1,0,2:T(4,128)S(1)} %copy.196), kind=kLoop, calls=%fused_computation.33 | loop fusion | flops 131072 | bytes 589312 | tf_op jit(solution)/shard_map/add | solution.py:24
  223.6 18.0 %all-gather.3 = f32[64,4,32]{2,1,0:T(4,128)S(1)} all-gather(f32[4,4,32]{2,1,0:T(4,128)S(1)} %copy.222), channel_id=5, replica_groups=mesh['ens'=2,'lon'=16] {'lon'}, dimensions={0}, use_global_device_ids=true | all-gather | bytes 34816 | tf_op jit(solution)/shard_map/all_gather | solution.py:34
  242.0 3.8 scatter_fusion.3
  254.5 6.7 %all-to-all-done = f32[16,2,512]{2,1,0:T(2,128)S(1)} async-done(((f32[16,2,512]{2,1,0:T(2,128)}), f32[16,2,512]{2,1,0:T(2,128)S(1)}, u32[]{:S(2)}, u32[]{:S(2)}) %all-to-all-start) | async-done | bytes 65568 | tf_op jit(solution)/shard_map/all_to_all | solution.py:82
  283.6 22.0 %all-gather.4 = f32[64,4,32]{2,1,0:T(4,128)S(1)} all-gather(f32[4,4,32]{2,1,0:T(4,128)S(1)} %copy.226), channel_id=6, replica_groups=mesh['ens'=2,'lon'=16] {'lon'}, dimensions={0}, use_global_device_ids=true | all-gather | bytes 34816 | tf_op jit(solution)/shard_map/all_gather | solution.py:34
  306.0 3.8 scatter_fusion.4
  309.8 4.5 broadcast_multiply_fusion.3
  318.1 7.0 %slice_multiply_fusion.7 = (f32[4,4,4,511]{2,1,3,0:T(4,128)}, f32[4,4,4,511]{2,1,3,0:T(4,128)}) fusion(f32[4,4,4,512]{2,1,3,0:T(4,128)} %scatter_fusion.4, f32[4,4,511]{1,0,2:T(4,128)} %slice.193, f32[4,4,511]{1,0,2:T(4,128)} %slice.195), kind=kLoop, calls=%fused_computation.44 | loop fusion | flops 65408 | bytes 588672 | tf_op jit(solution)/shard_map/mul | solution.py:46
  325.1 4.2 slice.191
  332.4 10.3 %fusion.1 = f32[4,4,4,512]{2,1,3,0:T(4,128)} fusion(f32[4,4,1,512]{2,1,3,0:T(4,128)} %copy.230, f32[4,4,3,512]{2,1,3,0:T(4,128)} %slice.191, f32[4,4,4,511]{2,1,3,0:T(4,128)} %get-tuple-element.30, f32[4,4,4,511]{2,1,3,0:T(4,128)} %get-tuple-element.29, f32[4,4,4,512]{2,1,3,0:T(4,128)} %scatter_fusion.4, f32[4,4,512]{1,0,2:T(4,128)S(1)} %copy.189), kind=kLoop, calls=%fused_computation.22 | loop fusion | flops 163840 | bytes 687616 | tf_op jit(solution)/shard_map/add | solution.py:50
  346.1 19.4 %all-gather.5 = f32[64,4,32]{2,1,0:T(4,128)S(1)} all-gather(f32[4,4,32]{2,1,0:T(4,128)S(1)} %copy.231), channel_id=7, replica_groups=mesh['ens'=2,'lon'=16] {'lon'}, dimensions={0}, use_global_device_ids=true | all-gather | bytes 34816 | tf_op jit(solution)/shard_map/all_gather | solution.py:34
  365.8 3.8 scatter_fusion.5
  369.6 4.5 broadcast_multiply_fusion
  378.0 7.0 %slice_multiply_fusion.5 = (f32[4,4,4,511]{2,1,3,0:T(4,128)}, f32[4,4,4,511]{2,1,3,0:T(4,128)}) fusion(f32[4,4,4,512]{2,1,3,0:T(4,128)} %scatter_fusion.5, f32[4,4,511]{1,0,2:T(4,128)} %slice.193, f32[4,4,511]{1,0,2:T(4,128)} %slice.195), kind=kLoop, calls=%fused_computation.42 | loop fusion | flops 65408 | bytes 588672 | tf_op jit(solution)/shard_map/mul | solution.py:46
  384.9 4.1 slice.197
  392.3 10.4 %fusion.3 = f32[4,4,4,512]{2,1,3,0:T(4,128)} fusion(f32[4,4,1,512]{2,1,3,0:T(4,128)} %copy.234, f32[4,4,3,512]{2,1,3,0:T(4,128)} %slice.197, f32[4,4,4,511]{2,1,3,0:T(4,128)} %get-tuple-element.28, f32[4,4,4,511]{2,1,3,0:T(4,128)} %get-tuple-element.27, f32[4,4,4,512]{2,1,3,0:T(4,128)} %scatter_fusion.5, f32[4,4,512]{1,0,2:T(4,128)S(1)} %copy.189), kind=kLoop, calls=%fused_computation.25 | loop fusion | flops 163840 | bytes 687616 | tf_op jit(solution)/shard_map/add | solution.py:50
  405.9 19.3 %all-gather.6 = f32[64,4,32]{2,1,0:T(4,128)S(1)} all-gather(f32[4,4,32]{2,1,0:T(4,128)S(1)} %copy.235), channel_id=8, replica_groups=mesh['ens'=2,'lon'=16] {'lon'}, dimensions={0}, use_global_device_ids=true | all-gather | bytes 34816 | tf_op jit(solution)/shard_map/all_gather | solution.py:34
  425.6 3.8 scatter_fusion.6
  429.4 4.5 broadcast_multiply_fusion.1
  437.9 7.1 %slice_multiply_fusion.3 = (f32[4,4,4,511]{2,1,3,0:T(4,128)}, f32[4,4,4,511]{2,1,3,0:T(4,128)}) fusion(f32[4,4,4,512]{2,1,3,0:T(4,128)} %scatter_fusion.6, f32[4,4,511]{1,0,2:T(4,128)} %slice.193, f32[4,4,511]{1,0,2:T(4,128)} %slice.195), kind=kLoop, calls=%fused_computation.40 | loop fusion | flops 65408 | bytes 588672 | tf_op jit(solution)/shard_map/mul | solution.py:46
  444.9 4.1 slice.203
  452.2 10.3 %fusion.5 = f32[4,4,4,512]{2,1,3,0:T(4,128)} fusion(f32[4,4,1,512]{2,1,3,0:T(4,128)} %copy.238, f32[4,4,3,512]{2,1,3,0:T(4,128)} %slice.203, f32[4,4,4,511]{2,1,3,0:T(4,128)} %get-tuple-element.26, f32[4,4,4,511]{2,1,3,0:T(4,128)} %get-tuple-element.25, f32[4,4,4,512]{2,1,3,0:T(4,128)} %scatter_fusion.6, f32[4,4,512]{1,0,2:T(4,128)S(1)} %copy.189), kind=kLoop, calls=%fused_computation.28 | loop fusion | flops 163840 | bytes 687616 | tf_op jit(solution)/shard_map/add | solution.py:50
  465.9 19.1 %all-gather.7 = f32[64,4,32]{2,1,0:T(4,128)S(1)} all-gather(f32[4,4,32]{2,1,0:T(4,128)S(1)} %copy.239), channel_id=9, replica_groups=mesh['ens'=2,'lon'=16] {'lon'}, dimensions={0}, use_global_device_ids=true | all-gather | bytes 34816 | tf_op jit(solution)/shard_map/all_gather | solution.py:34
  485.4 3.8 scatter_fusion.7
  489.2 4.5 broadcast_multiply_fusion.2
  493.6 3.6 copy.255
  498.0 6.9 %slice_multiply_fusion.1 = (f32[4,4,4,511]{2,1,3,0:T(4,128)}, f32[4,4,4,511]{2,1,3,0:T(4,128)}) fusion(f32[4,4,4,512]{2,1,3,0:T(4,128)} %scatter_fusion.7, f32[4,4,511]{1,0,2:T(4,128)S(1)} %copy-done.9, f32[4,4,511]{1,0,2:T(4,128)} %slice.195), kind=kLoop, calls=%fused_computation.38 | loop fusion | flops 65408 | bytes 588672 | tf_op jit(solution)/shard_map/mul | solution.py:46
  504.9 4.2 slice.209
  512.2 12.5 %fusion.8 = f32[4,4,4,512]{2,1,3,0:T(4,128)} fusion(f32[4,4,4,512]{2,1,3,0:T(4,128)} %copy.243, f32[4,4,1,512]{2,1,3,0:T(4,128)} %copy.242, f32[4,4,3,512]{2,1,3,0:T(4,128)} %slice.209, f32[4,4,4,511]{2,1,3,0:T(4,128)} %get-tuple-element.24, f32[4,4,4,511]{2,1,3,0:T(4,128)} %get-tuple-element.23, f32[4,4,4,512]{2,1,3,0:T(4,128)} %scatter_fusion.7, ...), kind=kLoop, calls=%fused_computation.32 | loop fusion | flops 196608 | bytes 818688 | tf_op jit(solution)/shard_map/add | solution.py:99
  524.7 4.4 copy.244
  (175 shorter events, 142.6 us)
Async XLA Ops:
  0.6 260.7 %copy-start = (f32[32,8,512]{2,1,0:T(8,128)S(1)}, f32[32,8,512]{2,1,0:T(8,128)}, u32[]{:S(2)}) copy-start(f32[32,8,512]{2,1,0:T(8,128)} %param.18) | copy-start | bytes 1572868
  1.7 14.7 %collective-permute-start = (f32[4,4,1,512]{3,1,2,0:T(4,128)S(1)}, f32[4,4,1,512]{3,1,2,0:T(4,128)S(1)}, u32[]{:S(2)}, u32[]{:S(2)}) collective-permute-start(f32[4,4,1,512]{3,1,2,0:T(4,128)S(1)} %slice.181), channel_id=1, source_target_pairs={{15,0},{0,1},{1,2},{2,3},{3,4},{4,5},{5,6},{6,7},{7,8},{8,9},{9,10... | collective-permute-start | bytes 98312 | tf_op jit(solution)/shard_map/ppermute | solution.py:13
  9.5 6.9 %copy-start.10 = (f32[4,4,4,512]{3,2,1,0:T(4,128)S(1)}, f32[4,4,4,512]{3,2,1,0:T(4,128)}, u32[]{:S(2)}) copy-start(f32[4,4,4,512]{3,2,1,0:T(4,128)} %param.11) | copy-start | bytes 393220
  9.5 6.9 %copy-start.15 = (f32[4,4]{1,0:T(4,128)S(1)}, f32[4,4]{1,0:T(4,128)}, u32[]{:S(2)}) copy-start(f32[4,4]{1,0:T(4,128)} %param.21) | copy-start | bytes 196
  57.4 6.5 %copy-start.2 = (f32[4,4,4,512]{2,1,3,0:T(4,128)S(1)}, f32[4,4,4,512]{2,1,3,0:T(4,128)}, u32[]{:S(2)}) copy-start(f32[4,4,4,512]{2,1,3,0:T(4,128)} %scatter_fusion) | copy-start | bytes 393220
  71.8 11.9 %collective-permute-start.1 = (f32[4,4,1,512]{3,1,2,0:T(4,128)S(1)}, f32[4,4,1,512]{3,1,2,0:T(4,128)S(1)}, u32[]{:S(2)}, u32[]{:S(2)}) collective-permute-start(f32[4,4,1,512]{3,1,2,0:T(4,128)S(1)} %copy.203), channel_id=1, source_target_pairs={{15,0},{0,1},{1,2},{2,3},{3,4},{4,5},{5,6},{6,7},{7,8},{8,9},{9,10... | collective-permute-start | bytes 98312 | tf_op jit(solution)/shard_map/ppermute | solution.py:13
  119.9 6.5 %copy-start.3 = (f32[4,4,4,512]{2,1,3,0:T(4,128)S(1)}, f32[4,4,4,512]{2,1,3,0:T(4,128)}, u32[]{:S(2)}) copy-start(f32[4,4,4,512]{2,1,3,0:T(4,128)} %scatter_fusion.1) | copy-start | bytes 393220
  134.3 11.8 %collective-permute-start.2 = (f32[4,4,1,512]{3,1,2,0:T(4,128)S(1)}, f32[4,4,1,512]{3,1,2,0:T(4,128)S(1)}, u32[]{:S(2)}, u32[]{:S(2)}) collective-permute-start(f32[4,4,1,512]{3,1,2,0:T(4,128)S(1)} %copy.210), channel_id=1, source_target_pairs={{15,0},{0,1},{1,2},{2,3},{3,4},{4,5},{5,6},{6,7},{7,8},{8,9},{9,10... | collective-permute-start | bytes 98312 | tf_op jit(solution)/shard_map/ppermute | solution.py:13
  183.1 6.5 %copy-start.4 = (f32[4,4,4,512]{2,1,3,0:T(4,128)S(1)}, f32[4,4,4,512]{2,1,3,0:T(4,128)}, u32[]{:S(2)}) copy-start(f32[4,4,4,512]{2,1,3,0:T(4,128)} %scatter_fusion.2) | copy-start | bytes 393220
  197.5 12.3 %collective-permute-start.3 = (f32[4,4,1,512]{3,1,2,0:T(4,128)S(1)}, f32[4,4,1,512]{3,1,2,0:T(4,128)S(1)}, u32[]{:S(2)}, u32[]{:S(2)}) collective-permute-start(f32[4,4,1,512]{3,1,2,0:T(4,128)S(1)} %copy.217), channel_id=1, source_target_pairs={{15,0},{0,1},{1,2},{2,3},{3,4},{4,5},{5,6},{6,7},{7,8},{8,9},{9,10... | collective-permute-start | bytes 98312 | tf_op jit(solution)/shard_map/ppermute | solution.py:13
  220.3 34.1 %copy-start.16 = (s32[16]{0:T(128)S(1)}, s32[16]{0:T(128)}, u32[]{:S(2)}) copy-start(s32[16]{0:T(128)} %param.17) | copy-start | bytes 196
  220.3 42.2 %copy-start.12 = (f32[32,8]{0,1:T(8,128)S(1)}, f32[32,8]{0,1:T(8,128)}, u32[]{:S(2)}) copy-start(f32[32,8]{0,1:T(8,128)} %param.20) | copy-start | bytes 3076
  220.3 42.2 %copy-start.13 = (f32[32,8]{0,1:T(8,128)S(1)}, f32[32,8]{0,1:T(8,128)}, u32[]{:S(2)}) copy-start(f32[32,8]{0,1:T(8,128)} %param.19) | copy-start | bytes 3076
  249.4 26.9 %copy-start.11 = (f32[4,4,4,512]{3,2,1,0:T(4,128)}, f32[4,4,4,512]{3,2,1,0:T(4,128)S(1)}, u32[]{:S(2)}) copy-start(f32[4,4,4,512]{3,2,1,0:T(4,128)S(1)} %copy.224) | copy-start | bytes 393220
  250.8 10.4 %all-to-all-start = ((f32[16,2,512]{2,1,0:T(2,128)}), f32[16,2,512]{2,1,0:T(2,128)S(1)}, u32[]{:S(2)}, u32[]{:S(2)}) async-start(f32[16,2,512]{2,1,0:T(2,128)} %all_to_all.16), calls=%async_computation | async-start | bytes 131072 | tf_op jit(solution)/shard_map/all_to_all | solution.py:82
  264.4 11.8 %copy-start.14 = (f32[32,8]{0,1:T(8,128)}, f32[32,8]{0,1:T(8,128)S(1)}, u32[]{:S(2)}) copy-start(f32[32,8]{0,1:T(8,128)S(1)} %subtract_multiply_fusion) | copy-start | bytes 3076
  265.7 10.5 %all-to-all-start.1 = ((f32[16,2,512]{2,1,0:T(2,128)}), f32[16,2,512]{2,1,0:T(2,128)S(1)}, u32[]{:S(2)}, u32[]{:S(2)}) async-start(f32[16,2,512]{2,1,0:T(2,128)} %all_to_all.19), calls=%async_computation.1 | async-start | bytes 131072 | tf_op jit(solution)/shard_map/all_to_all | solution.py:94
  317.8 7.2 %copy-start.6 = (f32[4,8,4,256]{2,1,3,0:T(8,128)S(1)}, f32[4,8,4,256]{2,1,3,0:T(8,128)}, u32[]{:S(2)}) copy-start(f32[4,8,4,256]{2,1,3,0:T(8,128)} %broadcast_multiply_fusion.3) | copy-start | bytes 393220
  317.8 11.4 %collective-permute-start.4 = (f32[4,4,1,512]{3,1,2,0:T(4,128)S(1)}, f32[4,4,1,512]{3,1,2,0:T(4,128)S(1)}, u32[]{:S(2)}, u32[]{:S(2)}) collective-permute-start(f32[4,4,1,512]{3,1,2,0:T(4,128)S(1)} %copy.252), channel_id=1, source_target_pairs={{1,0},{2,1},{3,2},{4,3},{5,4},{6,5},{7,6},{8,7},{9,8},{10,9},{11,1... | collective-permute-start | bytes 98312 | tf_op jit(solution)/shard_map/ppermute | solution.py:13
  377.6 7.3 %copy-start.7 = (f32[4,8,4,256]{2,1,3,0:T(8,128)S(1)}, f32[4,8,4,256]{2,1,3,0:T(8,128)}, u32[]{:S(2)}) copy-start(f32[4,8,4,256]{2,1,3,0:T(8,128)} %broadcast_multiply_fusion) | copy-start | bytes 393220
  377.6 11.5 %collective-permute-start.5 = (f32[4,4,1,512]{3,1,2,0:T(4,128)S(1)}, f32[4,4,1,512]{3,1,2,0:T(4,128)S(1)}, u32[]{:S(2)}, u32[]{:S(2)}) collective-permute-start(f32[4,4,1,512]{3,1,2,0:T(4,128)S(1)} %copy.253), channel_id=1, source_target_pairs={{1,0},{2,1},{3,2},{4,3},{5,4},{6,5},{7,6},{8,7},{9,8},{10,9},{11,1... | collective-permute-start | bytes 98312 | tf_op jit(solution)/shard_map/ppermute | solution.py:13
  437.4 7.5 %copy-start.8 = (f32[4,8,4,256]{2,1,3,0:T(8,128)S(1)}, f32[4,8,4,256]{2,1,3,0:T(8,128)}, u32[]{:S(2)}) copy-start(f32[4,8,4,256]{2,1,3,0:T(8,128)} %broadcast_multiply_fusion.1) | copy-start | bytes 393220
  437.4 11.6 %collective-permute-start.6 = (f32[4,4,1,512]{3,1,2,0:T(4,128)S(1)}, f32[4,4,1,512]{3,1,2,0:T(4,128)S(1)}, u32[]{:S(2)}, u32[]{:S(2)}) collective-permute-start(f32[4,4,1,512]{3,1,2,0:T(4,128)S(1)} %copy.254), channel_id=1, source_target_pairs={{1,0},{2,1},{3,2},{4,3},{5,4},{6,5},{7,6},{8,7},{9,8},{10,9},{11,1... | collective-permute-start | bytes 98312 | tf_op jit(solution)/shard_map/ppermute | solution.py:13
  493.6 4.3 copy-start.9
  497.3 7.6 %copy-start.5 = (f32[4,8,4,256]{2,1,3,0:T(8,128)S(1)}, f32[4,8,4,256]{2,1,3,0:T(8,128)}, u32[]{:S(2)}) copy-start(f32[4,8,4,256]{2,1,3,0:T(8,128)} %broadcast_multiply_fusion.2) | copy-start | bytes 393220
  497.3 11.8 %collective-permute-start.7 = (f32[4,4,1,512]{3,1,2,0:T(4,128)S(1)}, f32[4,4,1,512]{3,1,2,0:T(4,128)S(1)}, u32[]{:S(2)}, u32[]{:S(2)}) collective-permute-start(f32[4,4,1,512]{3,1,2,0:T(4,128)S(1)} %copy.255), channel_id=1, source_target_pairs={{1,0},{2,1},{3,2},{4,3},{5,4},{6,5},{7,6},{8,7},{9,8},{10,9},{11,1... | collective-permute-start | bytes 98312 | tf_op jit(solution)/shard_map/ppermute | solution.py:13
  512.2 16.9 %copy-start.1 = (f32[32,8,512]{2,1,0:T(8,128)S(1)}, f32[32,8,512]{2,1,0:T(8,128)}, u32[]{:S(2)}) copy-start(f32[32,8,512]{2,1,0:T(8,128)} %param.18) | copy-start | bytes 1572868
